TPU v7x, 512 devices: a whole 4x8x8 slice. The times are simulated.
512 devices in a mesh: dev: 128 (over y, z, core), band: 4 (over x).
Axes of the slice: x: 4, y: 8, z: 8, core: 2. Of those that a mesh axis runs over, the one named last changes fastest.
Arguments:
- embeddings: bfloat16 [1048576, 1024], P(('band', 'dev')), parts along dimension 0, may hold values from -6 to 6
- pair_local: int32 [512], P(('band', 'dev')), parts along dimension 0, may hold values from 0 to 1
- pair_remote: int32 [512], P(('band', 'dev')), parts along dimension 0, may hold values from 0 to 1
- pair_live: int32 [512], P(('band', 'dev')), parts along dimension 0, may hold values from 0 to 1, as said below
Outputs:
- best: float32 [1024, 1024], P(('band', 'dev')), parts along dimension 0
There are 4 independent parts, one for each index of `band`. A program takes and returns all parts, laid end to end along the dimension named above; each array names one. Nothing has to cross between parts.
Inputs may be any that keep to these rules, and one draw needn't show every extreme that they name: pair_live is 0 wherever the partner device index i + o would reach 128 or beyond; all slots of device 0 are live.
All inputs are finite; a program needn't handle non-finite values.
Results may differ from a plain program's by a relative error of at most 0.0013.
Values may be sent and summed in bfloat16 or wider, within the bound.
A program may use at most 64 MiB of HBM per device.

v0:
```python
import jax
import jax.numpy as jnp
from jax import lax
from jax.sharding import PartitionSpec as P

BLK = 1024
SPAN = 2
CAP = 1


def from_behind(value, axis, by):
    count = lax.axis_size(axis)
    pairs = [(i, i + by) for i in range(count) if 0 <= i + by < count]
    return lax.ppermute(value, axis, pairs)


def spread_max(values, targets, count):
    chosen = targets[:, None] == jnp.arange(count, dtype=jnp.int32)[None, :]
    return jnp.max(jnp.where(chosen[:, :, None], values[:, None, :], -2.0), axis=0)


def local(embeddings, pair_local, pair_remote, pair_live):
    rows = embeddings.astype(jnp.float32)
    normed = (rows * lax.rsqrt(jnp.sum(rows * rows, axis=1, keepdims=True) + 1e-06)).astype(
        jnp.bfloat16
    )
    count = embeddings.shape[0] // BLK
    normed = normed.reshape(count, BLK, embeddings.shape[1])
    local_ids = pair_local.reshape(SPAN - 1, CAP)
    remote_ids = pair_remote.reshape(SPAN - 1, CAP)
    live_ids = pair_live.reshape(SPAN - 1, CAP)
    position = lax.axis_index("dev")
    own_gram = jnp.einsum("bre,bse->brs", normed, normed, preferred_element_type=jnp.float32)
    diagonal = jnp.eye(BLK, dtype=bool)
    best = jnp.max(jnp.where(diagonal[None], -2.0, own_gram), axis=2)
    wanted_here = remote_ids[0]
    ahead = from_behind(normed, "dev", -1)
    partner = jnp.take(ahead, wanted_here, axis=0)
    mine = jnp.take(normed, local_ids[0], axis=0)
    gram = jnp.einsum("cre,cse->crs", mine, partner, preferred_element_type=jnp.float32)
    alive = live_ids[0][:, None] > 0
    row_best = jnp.where(alive, jnp.max(gram, axis=2), -2.0)
    col_best = jnp.where(alive, jnp.max(gram, axis=1), -2.0)
    best = jnp.maximum(best, spread_max(row_best, local_ids[0], count))
    outgoing = spread_max(col_best, wanted_here, count)
    returned = from_behind(outgoing, "dev", 1)
    best = jnp.maximum(best, jnp.where(position >= 1, returned, -2.0))
    return best


def solution(mesh):
    placed = (P(("band", "dev"), None), P(("band", "dev")), P(("band", "dev")), P(("band", "dev")))
    return jax.shard_map(
        local, mesh=mesh, in_specs=placed, out_specs=P(("band", "dev"), None), check_vma=False
    )
```

profile of v0, /device:TPU:38, one launch (start us, length us, event | category | flops | bytes accessed | tf_op | source)
XLA Modules:
  0.0 76.6 jit_solution(13762479665908482182)
XLA Ops:
  0.0 0.0 copy-start
  0.0 3.2 %fusion = f32[2048]{0:T(1024)S(1)} fusion(bf16[2048,1024]{1,0:T(8,128)(2,1)} %param.6), kind=kLoop, calls=%fused_computation.2 | loop fusion | flops 6289408 | bytes 4202496 | tf_op jit(solution)/shard_map/reduce_sum | solution.py:24
  3.2 0.2 copy-done
  3.5 2.7 %fusion.1 = bf16[2048,1024]{1,0:T(8,128)(2,1)} fusion(bf16[2048,1024]{1,0:T(8,128)(2,1)S(1)} %copy-done, f32[2048]{0:T(1024)S(1)} %add_rsqrt_fusion), kind=kLoop, calls=%fused_computation.3 | loop fusion | flops 6291456 | bytes 8396800 | tf_op jit(solution)/shard_map/convert_element_type | solution.py:24
  6.1 10.3 %collective-permute-start = (bf16[2,1024,1024]{2,1,0:T(8,128)(2,1)}, bf16[2,1024,1024]{2,1,0:T(8,128)(2,1)}, u32[]{:S(2)}, u32[]{:S(2)}) collective-permute-start(bf16[2,1024,1024]{2,1,0:T(8,128)(2,1)} %bitcast), channel_id=1, source_target_pairs={{4,0},{8,4},{12,8},{16,12},{20,16},{24,20},{28,24},{32,28},{36,32}... | collective-permute-start | bytes 12582920 | tf_op jit(solution)/shard_map/ppermute | solution.py:14
  18.4 0.3 iota_compare_fusion
  18.7 8.4 %select_reduce_fusion = f32[2,1024]{1,0:T(2,128)S(1)} fusion(pred[1024,1024]{0,1:T(8,128)(4,1)S(1)} %iota_compare_fusion, bf16[2,1024,1024]{2,1,0:T(8,128)(2,1)} %bitcast), kind=kOutput, calls=%fused_computation.4 | convolution fusion | flops 4299159552 | bytes 5251072 | tf_op jit(solution)/shard_map/bre,bse->brs/dot_general | solution.py:33
  27.1 35.6 %collective-permute-done = bf16[2,1024,1024]{2,1,0:T(8,128)(2,1)} collective-permute-done((bf16[2,1024,1024]{2,1,0:T(8,128)(2,1)}, bf16[2,1024,1024]{2,1,0:T(8,128)(2,1)}, u32[]{:S(2)}, u32[]{:S(2)}) %collective-permute-start) | collective-permute-done | bytes 4194336 | tf_op jit(solution)/shard_map/ppermute | solution.py:14
  62.7 4.7 %fusion.14 = (f32[1024]{0:T(1024)S(1)}, f32[1024]{0:T(1024)S(1)}) fusion(bf16[2,1024,1024]{2,1,0:T(8,128)(2,1)} %collective-permute-done, s32[]{:T(128)} %bitcast.7, pred[]{:T(512)} %bitcast.6, bf16[2,1024,1024]{2,1,0:T(8,128)(2,1)} %bitcast, s32[]{:T(128)} %bitcast.4, pred[]{:T(512)} %bitcast.3), kind=kOutput, calls=%fused_computation.25 | convolution fusion | flops 2151675904 | bytes 4204544 | tf_op jit(solution)/shard_map/cre,cse->crs/dot_general | solution.py:40
  67.4 0.1 broadcast_select_fusion
  67.5 1.9 %collective-permute-start.1 = (f32[2,1024]{1,0:T(2,128)S(1)}, f32[2,1024]{1,0:T(2,128)S(1)}, u32[]{:S(2)}, u32[]{:S(2)}) collective-permute-start(f32[2,1024]{1,0:T(2,128)S(1)} %broadcast_select_fusion), channel_id=1, source_target_pairs={{0,4},{4,8},{8,12},{12,16},{16,20},{20,24},{24,28},{28,32},{32,36}... | collective-permute-start | bytes 24584 | tf_op jit(solution)/shard_map/ppermute | solution.py:14
  69.4 6.5 %collective-permute-done.1 = f32[2,1024]{1,0:T(2,128)S(1)} collective-permute-done((f32[2,1024]{1,0:T(2,128)S(1)}, f32[2,1024]{1,0:T(2,128)S(1)}, u32[]{:S(2)}, u32[]{:S(2)}) %collective-permute-start.1) | collective-permute-done | bytes 8224 | tf_op jit(solution)/shard_map/ppermute | solution.py:14
  75.9 0.7 select_maximum_fusion
  (5 shorter events, 0.0 us)
Async XLA Ops:
  0.0 3.4 %copy-start = (bf16[2048,1024]{1,0:T(8,128)(2,1)S(1)}, bf16[2048,1024]{1,0:T(8,128)(2,1)}, u32[]{:S(2)}) copy-start(bf16[2048,1024]{1,0:T(8,128)(2,1)} %param.6) | copy-start | bytes 12582916
  6.1 56.6 %collective-permute-start = (bf16[2,1024,1024]{2,1,0:T(8,128)(2,1)}, bf16[2,1024,1024]{2,1,0:T(8,128)(2,1)}, u32[]{:S(2)}, u32[]{:S(2)}) collective-permute-start(bf16[2,1024,1024]{2,1,0:T(8,128)(2,1)} %bitcast), channel_id=1, source_target_pairs={{4,0},{8,4},{12,8},{16,12},{20,16},{24,20},{28,24},{32,28},{36,32}... | collective-permute-start | bytes 12582920 | tf_op jit(solution)/shard_map/ppermute | solution.py:14
  67.5 8.5 %collective-permute-start.1 = (f32[2,1024]{1,0:T(2,128)S(1)}, f32[2,1024]{1,0:T(2,128)S(1)}, u32[]{:S(2)}, u32[]{:S(2)}) collective-permute-start(f32[2,1024]{1,0:T(2,128)S(1)} %broadcast_select_fusion), channel_id=1, source_target_pairs={{0,4},{4,8},{8,12},{12,16},{16,20},{20,24},{24,28},{28,32},{32,36}... | collective-permute-start | bytes 24584 | tf_op jit(solution)/shard_map/ppermute | solution.py:14
where the time goes:
time: 76.7 us; the launch traced here: 76.6 us
  waiting for transfers between devices  42.1 us (55%)
  matrix products  13.1 us (17%)
  starting transfers between devices  12.2 us (16%)
  other arithmetic  6.98 us (9%)
  between operations  2.04 us (3%)
    ppermute x2, waiting for transfers between devices, from_behind(): return lax.ppermute(value, axis, pairs)  42.1 us
    ppermute x2, starting transfers between devices, from_behind(): return lax.ppermute(value, axis, pairs)  12.2 us
    dot_general x1, matrix products, local(): jnp.einsum('bre,bse->brs', normed, normed, preferred_element_type=jnp.flo...  8.4 us
    dot_general x1, matrix products, local(): jnp.einsum('cre,cse->crs', mine, partner, preferred_element_type=jnp.floa...  4.66 us
    reduce_sum x1, other arithmetic, local(): jnp.sum(rows * rows, axis=1, keepdims=True) + 1e-06  3.22 us
    convert_element_type x1, other arithmetic, local(): (rows * lax.rsqrt(jnp.sum(rows * rows, axis=1, keepdims=True) + 1e-06)).a...  2.67 us
  transfers between devices with their start and end apart: 2, of which 2 were waited for; matrix products, arithmetic and copies ran while one was open for 11% of the time, Pallas kernels for 0%

commit v1 on v0

v1 whole, which is shorter than its diff:
```python
import functools

import jax
import jax.numpy as jnp
from jax import lax
from jax.experimental import pallas as pl
from jax.experimental.pallas import tpu as pltpu
from jax.sharding import PartitionSpec as P

BLK = 1024
D = 1024
ROUNDS = 8
CHUNK = BLK // ROUNDS
DIRECT = 64
RELAY = 32
SPLIT_ROUNDS = 7
OWN = 256
LINE = 8
PAIR = 256
MESH = pl.DeviceIdType.MESH


def kernel(
    n_dev,
    n_band,
    local_ref,
    remote_ref,
    live_ref,
    x_hbm,
    best_ref,
    sent_ref,
    xn,
    send_buf,
    recv_buf,
    relay_buf,
    meta_out,
    meta_in,
    ret_out,
    ret_in,
    own_acc,
    pair_acc,
    load_sem,
    meta_sem,
    ret_sem,
    direct_send,
    direct_recv,
    leg1_send,
    leg1_recv,
    leg2_send,
    leg2_recv,
):
    d = lax.axis_index("dev")
    b = lax.axis_index("band")
    c = d % 2
    odd = b % 2
    step = 1 - 2 * odd
    is_s = c == 1 - odd
    is_r = c == odd
    crosses = jnp.where(c == 1, d < n_dev - 1, d > 0)
    s_cross = jnp.logical_and(is_s, crosses)
    r_cross = jnp.logical_and(is_r, crosses)
    other = d + 1 - 2 * c
    across = jnp.where(crosses, d - 1 + 2 * c, other)
    target = jnp.clip(d + step, 0, n_dev - 1)
    source = jnp.clip(d - step, 0, n_dev - 1)
    bands = (lax.rem(b + 1, n_band), lax.rem(b + n_band - 1, n_band))
    has_target = jnp.logical_or(is_r, crosses)
    has_source = jnp.logical_or(is_s, crosses)

    def load(t):
        rows = pl.ds(pl.multiple_of(t * CHUNK, CHUNK), CHUNK)
        return pltpu.make_async_copy(x_hbm.at[:, rows], xn.at[:, rows], load_sem.at[t])

    for t in range(ROUNDS):
        load(t).start()

    barrier = pltpu.get_barrier_semaphore()

    def greet(dev, band):
        pl.semaphore_signal(barrier, inc=1, device_id=(dev, band), device_id_type=MESH)

    greet(other, b)

    @pl.when(crosses)
    def _():
        greet(across, b)
        for band in bands:
            greet(d, band)

    @pl.when(r_cross)
    def _():
        for band in bands:
            greet(across, band)

    own_acc[...] = jnp.full(own_acc.shape, -2.0, jnp.float32)
    pair_acc[...] = jnp.full(pair_acc.shape, -2.0, jnp.float32)

    def normalize(t, carry):
        rows = pl.ds(pl.multiple_of(t * CHUNK, CHUNK), CHUNK)
        load(t).wait()
        for k in range(2):
            values = xn[k, rows].astype(jnp.float32)
            scale = lax.rsqrt(jnp.sum(values * values, axis=1, keepdims=True) + 1e-06)
            xn[k, rows] = (values * scale).astype(jnp.bfloat16)
        return carry

    early = jnp.where(d // 2 % LINE == LINE - 1, 0, ROUNDS)
    lax.fori_loop(0, early, normalize, 0)

    row = lax.broadcasted_iota(jnp.int32, (8, 128), 0)
    meta_out[...] = jnp.where(row == 0, remote_ref[0], live_ref[0])

    def own(t, carry):
        k = t % 2
        first = pl.multiple_of(t // 2 * OWN, OWN)
        gram = lax.dot_general(
            xn[k, pl.ds(first, OWN)],
            xn[k],
            (((1,), (1,)), ((), ())),
            preferred_element_type=jnp.float32,
        )
        rows = lax.broadcasted_iota(jnp.int32, gram.shape, 0) + first
        columns = lax.broadcasted_iota(jnp.int32, gram.shape, 1)
        gram = jnp.where(rows == columns, -2.0, gram)
        own_acc[k] = jnp.maximum(own_acc[k], jnp.max(gram.reshape(OWN // 8, 8, BLK), axis=0))
        return carry

    lax.fori_loop(0, early, own, 0)

    waits = 1 + jnp.where(crosses, 3, 0) + jnp.where(r_cross, 2, 0)
    pl.semaphore_wait(barrier, waits)

    meta_copy = pltpu.make_async_remote_copy(
        src_ref=meta_out,
        dst_ref=meta_in,
        send_sem=meta_sem.at[0],
        recv_sem=meta_sem.at[1],
        device_id=(jnp.minimum(d + 1, n_dev - 1), b),
        device_id_type=MESH,
    )

    @pl.when(d < n_dev - 1)
    def _():
        meta_copy.start()

    def piece(t, start, size):
        return pl.ds(pl.multiple_of(t * CHUNK + start, 16), size)

    def direct(t, size):
        rows = piece(t, 0, size)
        return pltpu.make_async_remote_copy(
            src_ref=send_buf.at[rows],
            dst_ref=recv_buf.at[rows],
            send_sem=direct_send.at[t],
            recv_sem=direct_recv.at[t],
            device_id=(target, b),
            device_id_type=MESH,
        )

    def relay_rows(t, side):
        return piece(t, DIRECT + side * RELAY, RELAY)

    def leg1(t, side):
        return pltpu.make_async_remote_copy(
            src_ref=send_buf.at[relay_rows(t, side)],
            dst_ref=relay_buf.at[side, pl.ds(pl.multiple_of(t * RELAY, RELAY), RELAY)],
            send_sem=leg1_send.at[side, t],
            recv_sem=leg1_recv.at[side, t],
            device_id=(d, bands[side]),
            device_id_type=MESH,
        )

    def leg2(t, side):
        return pltpu.make_async_remote_copy(
            src_ref=relay_buf.at[side, pl.ds(pl.multiple_of(t * RELAY, RELAY), RELAY)],
            dst_ref=recv_buf.at[relay_rows(t, side)],
            send_sem=leg2_send.at[side, t],
            recv_sem=leg2_recv.at[side, t],
            device_id=(across, bands[1 - side]),
            device_id_type=MESH,
        )

    def forward(t):
        for side in range(2):
            leg1(t, side).wait_recv()
            leg2(t, side).start()

    def send(t, index):
        rows = piece(t, 0, CHUNK)
        send_buf[rows] = jnp.where(index == 0, xn[0, rows], xn[1, rows])

        @pl.when(is_r)
        def _():
            direct(t, CHUNK).start()

        @pl.when(s_cross)
        def _():
            @pl.when(t < SPLIT_ROUNDS)
            def _():
                for side in range(2):
                    leg1(t, side).start()
                direct(t, DIRECT).start()

            @pl.when(t >= SPLIT_ROUNDS)
            def _():
                direct(t, CHUNK).start()

    def send_all(index):
        def body(t, carry):
            @pl.when(t >= early)
            def _():
                normalize(t, 0)

            send(t, index)
            return carry

        lax.fori_loop(0, ROUNDS, body, 0)

    def learn():
        @pl.when(d > 0)
        def _():
            meta_copy.wait_recv()

        @pl.when(d == 0)
        def _():
            meta_in[...] = jnp.zeros_like(meta_in)

    @pl.when(odd == 0)
    def _():
        send_all(local_ref[0])
        learn()

    @pl.when(odd == 1)
    def _():
        learn()
        send_all(meta_in[0, 0])

    before_remote = meta_in[0, 0]
    before_live = meta_in[1, 0]
    forwards = odd == 0
    send_index = jnp.where(forwards, local_ref[0], before_remote)
    send_live = jnp.where(forwards, live_ref[0], before_live)
    keep_index = jnp.where(forwards, before_remote, local_ref[0])
    keep_live = jnp.where(forwards, before_live, live_ref[0])

    def relay(t, carry):
        @pl.when(t >= early)
        def _():
            own(t, 0)

        @pl.when(jnp.logical_and(r_cross, t < SPLIT_ROUNDS))
        def _():
            forward(t)

        return carry

    lax.fori_loop(0, ROUNDS, relay, 0)

    def arrive(t):
        @pl.when(jnp.logical_or(is_s, t >= SPLIT_ROUNDS))
        def _():
            direct(t, CHUNK).wait_recv()

        @pl.when(jnp.logical_and(is_r, t < SPLIT_ROUNDS))
        def _():
            direct(t, DIRECT).wait_recv()
            for side in range(2):
                leg2(t, side).wait_recv()

    def pair(t):
        rows = pl.ds(pl.multiple_of(t * PAIR, PAIR), PAIR)
        gram = lax.dot_general(
            recv_buf[rows],
            xn[keep_index],
            (((1,), (1,)), ((), ())),
            preferred_element_type=jnp.float32,
        )
        pair_acc[...] = jnp.maximum(
            pair_acc[...], jnp.max(gram.reshape(PAIR // 8, 8, BLK), axis=0)
        )
        narrow = gram[:, :128]
        for j in range(1, BLK // 128):
            narrow = jnp.maximum(narrow, gram[:, j * 128 : (j + 1) * 128])
        for j in range(PAIR // 128):
            part = jnp.max(narrow[j * 128 : (j + 1) * 128].T, axis=0, keepdims=True)
            ret_out[pl.ds(t * (PAIR // 128) + j, 1)] = part

    def compare(t, carry):
        for j in range(PAIR // CHUNK):
            arrive(t * (PAIR // CHUNK) + j)
        pair(t)
        return carry

    @pl.when(has_source)
    def _():
        lax.fori_loop(0, BLK // PAIR, compare, 0)

    ret_copy = pltpu.make_async_remote_copy(
        src_ref=ret_out,
        dst_ref=ret_in,
        send_sem=ret_sem.at[0],
        recv_sem=ret_sem.at[1],
        device_id=(source, b),
        device_id_type=MESH,
    )

    @pl.when(has_source)
    def _():
        ret_copy.start()

    @pl.when(has_target)
    def _():
        ret_copy.wait_recv()

    @pl.when(jnp.logical_not(has_target))
    def _():
        ret_in[...] = jnp.full(ret_in.shape, -2.0, jnp.float32)

    kept = jnp.max(pair_acc[...], axis=0, keepdims=True)
    kept = jnp.where(keep_live > 0, kept, -2.0)
    sent = jnp.concatenate([ret_in[t : t + 1] for t in range(ROUNDS)], axis=1)
    sent = jnp.where(send_live > 0, sent, -2.0)
    for k in range(2):
        best = jnp.max(own_acc[k], axis=0, keepdims=True)
        best_ref[k : k + 1] = jnp.maximum(best, jnp.where(keep_index == k, kept, -2.0))
        sent_ref[k : k + 1] = jnp.where(send_index == k, sent, -2.0)

    @pl.when(d < n_dev - 1)
    def _():
        meta_copy.wait_send()

    @pl.when(has_source)
    def _():
        ret_copy.wait_send()

    def drain(t, carry):
        @pl.when(jnp.logical_or(is_r, jnp.logical_and(crosses, t >= SPLIT_ROUNDS)))
        def _():
            direct(t, CHUNK).wait_send()

        @pl.when(jnp.logical_and(s_cross, t < SPLIT_ROUNDS))
        def _():
            direct(t, DIRECT).wait_send()
            for side in range(2):
                leg1(t, side).wait_send()

        @pl.when(jnp.logical_and(r_cross, t < SPLIT_ROUNDS))
        def _():
            for side in range(2):
                leg2(t, side).wait_send()

        return carry

    lax.fori_loop(0, ROUNDS, drain, 0)


def solution(mesh):
    n_dev, n_band = mesh.shape["dev"], mesh.shape["band"]
    dma = pltpu.SemaphoreType.DMA

    def local(embeddings, pair_local, pair_remote, pair_live):
        blocks = embeddings.reshape(2, BLK, D)
        best, sent = pl.pallas_call(
            functools.partial(kernel, n_dev, n_band),
            out_shape=[jax.ShapeDtypeStruct((2, BLK), jnp.float32)] * 2,
            in_specs=[pl.BlockSpec(memory_space=pltpu.SMEM)] * 3
            + [pl.BlockSpec(memory_space=pl.ANY)],
            out_specs=[pl.BlockSpec(memory_space=pltpu.VMEM)] * 2,
            scratch_shapes=[
                pltpu.VMEM((2, BLK, D), jnp.bfloat16),
                pltpu.VMEM((BLK, D), jnp.bfloat16),
                pltpu.VMEM((BLK, D), jnp.bfloat16),
                pltpu.VMEM((2, ROUNDS * RELAY, D), jnp.bfloat16),
                pltpu.VMEM((8, 128), jnp.int32),
                pltpu.VMEM((8, 128), jnp.int32),
                pltpu.VMEM((ROUNDS, CHUNK), jnp.float32),
                pltpu.VMEM((ROUNDS, CHUNK), jnp.float32),
                pltpu.VMEM((2, 8, BLK), jnp.float32),
                pltpu.VMEM((8, BLK), jnp.float32),
                dma((ROUNDS,)),
                dma((2,)),
                dma((2,)),
                dma((ROUNDS,)),
                dma((ROUNDS,)),
                dma((2, ROUNDS)),
                dma((2, ROUNDS)),
                dma((2, ROUNDS)),
                dma((2, ROUNDS)),
            ],
            compiler_params=pltpu.CompilerParams(
                collective_id=1, has_side_effects=True, vmem_limit_bytes=52 << 20
            ),
            cost_estimate=pl.CostEstimate(
                flops=6 * BLK * BLK * D, bytes_accessed=4 * BLK * D, transcendentals=0
            ),
        )(pair_local, pair_remote, pair_live, blocks)
        return jnp.maximum(best, sent)

    placed = (P(("band", "dev"), None), P(("band", "dev")), P(("band", "dev")), P(("band", "dev")))
    return jax.shard_map(
        local, mesh=mesh, in_specs=placed, out_specs=P(("band", "dev"), None), check_vma=False
    )
```

time: 76.7 us -> 38 us (0.50)
  the two profiles are of different devices: /device:TPU:38 before, /device:TPU:34 now
where the time goes in v1:
time: 38 us; the launch traced here: 37.9 us
  Pallas kernels  35.4 us (93%)
  between operations  1.95 us (5%)
  other arithmetic  0.6 us (2%)
    pallas_call x1, Pallas kernels, local(): pl.pallas_call(functools.partial(kernel, n_dev, n_band), out_shape=[jax.S...  35.4 us

profile of v1, /device:TPU:34, one launch (start us, length us, event | category | flops | bytes accessed | tf_op | source)
XLA Modules:
  0.0 37.9 jit_solution(3375169085918719877)
XLA Ops:
  1.9 35.4 %shard_map.46 = (f32[2,1024]{1,0:T(2,128)S(1)}, f32[2,1024]{1,0:T(2,128)S(1)}) custom-call(s32[1]{0:T(128)S(6)} %copy.5.local_ref, s32[1]{0:T(128)S(6)} %copy.6.remote_ref, s32[1]{0:T(128)S(6)} %copy.7.live_ref, bf16[2,1024,1024]{2,1,0:T(8,128)(2,1)} %bitcast.1), custom_call_target="tpu_custom_call" | custom-call | flops 6442450944 | bytes 4194304 | tf_op jit(solution)/shard_map/pallas_call | solution.py:363
  37.3 0.6 %max.3 = f32[2,1024]{1,0:T(2,128)} maximum(f32[2,1024]{1,0:T(2,128)S(1)} %get-tuple-element.7, f32[2,1024]{1,0:T(2,128)S(1)} %get-tuple-element.8) | non-fusion elementwise | flops 2048 | bytes 24576 | tf_op jit(solution)/shard_map/max | solution.py:397

commit v2 on v1

--- a/solution.py
+++ b/solution.py
@@ -13,9 +13,11 @@
 CHUNK = BLK // ROUNDS
 DIRECT = 64
 RELAY = 32
-SPLIT_ROUNDS = 7
+SPLIT_ROUNDS = 6
 OWN = 256
 LINE = 8
+AHEAD = 6
+BEFORE = 4
 PAIR = 256
 MESH = pl.DeviceIdType.MESH
 
@@ -84,12 +86,11 @@
     @pl.when(crosses)
     def _():
         greet(across, b)
+
+    @pl.when(r_cross)
+    def _():
         for band in bands:
             greet(d, band)
-
-    @pl.when(r_cross)
-    def _():
-        for band in bands:
             greet(across, band)
 
     own_acc[...] = jnp.full(own_acc.shape, -2.0, jnp.float32)
@@ -104,7 +105,9 @@
             xn[k, rows] = (values * scale).astype(jnp.bfloat16)
         return carry
 
-    early = jnp.where(d // 2 % LINE == LINE - 1, 0, ROUNDS)
+    first = d // 2 % LINE == 0
+    early = jnp.where(first, ROUNDS, 0)
+    before = jnp.where(first, BEFORE, 0)
     lax.fori_loop(0, early, normalize, 0)
 
     row = lax.broadcasted_iota(jnp.int32, (8, 128), 0)
@@ -112,22 +115,22 @@
 
     def own(t, carry):
         k = t % 2
-        first = pl.multiple_of(t // 2 * OWN, OWN)
+        start = pl.multiple_of(t // 2 * OWN, OWN)
         gram = lax.dot_general(
-            xn[k, pl.ds(first, OWN)],
+            xn[k, pl.ds(start, OWN)],
             xn[k],
             (((1,), (1,)), ((), ())),
             preferred_element_type=jnp.float32,
         )
-        rows = lax.broadcasted_iota(jnp.int32, gram.shape, 0) + first
+        rows = lax.broadcasted_iota(jnp.int32, gram.shape, 0) + start
         columns = lax.broadcasted_iota(jnp.int32, gram.shape, 1)
         gram = jnp.where(rows == columns, -2.0, gram)
         own_acc[k] = jnp.maximum(own_acc[k], jnp.max(gram.reshape(OWN // 8, 8, BLK), axis=0))
         return carry
 
-    lax.fori_loop(0, early, own, 0)
-
-    waits = 1 + jnp.where(crosses, 3, 0) + jnp.where(r_cross, 2, 0)
+    lax.fori_loop(0, before, own, 0)
+
+    waits = 1 + jnp.where(crosses, 3, 0)
     pl.semaphore_wait(barrier, waits)
 
     meta_copy = pltpu.make_async_remote_copy(
@@ -225,15 +228,34 @@
         def _():
             meta_in[...] = jnp.zeros_like(meta_in)
 
+    def relay(t, carry):
+        @pl.when(t >= before)
+        def _():
+            own(t, 0)
+
+        @pl.when(jnp.logical_and(r_cross, t < SPLIT_ROUNDS))
+        def _():
+            forward(t)
+
+        return carry
+
+    ahead = jnp.where(jnp.logical_and(is_r, jnp.logical_and(odd == 1, first)), AHEAD, 0)
+    lax.fori_loop(0, ahead, relay, 0)
+
     @pl.when(odd == 0)
     def _():
         send_all(local_ref[0])
-        learn()
 
     @pl.when(odd == 1)
     def _():
         learn()
         send_all(meta_in[0, 0])
+
+    lax.fori_loop(ahead, ROUNDS, relay, 0)
+
+    @pl.when(odd == 0)
+    def _():
+        learn()
 
     before_remote = meta_in[0, 0]
     before_live = meta_in[1, 0]
@@ -242,19 +264,6 @@
     send_live = jnp.where(forwards, live_ref[0], before_live)
     keep_index = jnp.where(forwards, before_remote, local_ref[0])
     keep_live = jnp.where(forwards, before_live, live_ref[0])
-
-    def relay(t, carry):
-        @pl.when(t >= early)
-        def _():
-            own(t, 0)
-
-        @pl.when(jnp.logical_and(r_cross, t < SPLIT_ROUNDS))
-        def _():
-            forward(t)
-
-        return carry
-
-    lax.fori_loop(0, ROUNDS, relay, 0)
 
     def arrive(t):
         @pl.when(jnp.logical_or(is_s, t >= SPLIT_ROUNDS))

time: 38 us -> 37.5 us (0.987)
  Pallas kernels: 35.4 us -> 34.8 us
    pallas_call x1, Pallas kernels: 35.4 us -> 34.8 us  [local(): pl.pallas_call(functools.partial(kernel, n_dev, n_band), out_shape=[jax.S...]
where the time goes in v2:
time: 37.5 us; the launch traced here: 37.3 us
  Pallas kernels  34.8 us (93%)
  between operations  1.95 us (5%)
  other arithmetic  0.6 us (2%)
    pallas_call x1, Pallas kernels, local(): pl.pallas_call(functools.partial(kernel, n_dev, n_band), out_shape=[jax.S...  34.8 us

profile of v2, /device:TPU:34, one launch (start us, length us, event | category | flops | bytes accessed | tf_op | source)
XLA Modules:
  0.0 37.3 jit_solution(16610993144038375256)
XLA Ops:
  1.9 34.8 %shard_map.46 = (f32[2,1024]{1,0:T(2,128)S(1)}, f32[2,1024]{1,0:T(2,128)S(1)}) custom-call(s32[1]{0:T(128)S(6)} %copy.5.local_ref, s32[1]{0:T(128)S(6)} %copy.6.remote_ref, s32[1]{0:T(128)S(6)} %copy.7.live_ref, bf16[2,1024,1024]{2,1,0:T(8,128)(2,1)} %bitcast.1), custom_call_target="tpu_custom_call" | custom-call | flops 6442450944 | bytes 4194304 | tf_op jit(solution)/shard_map/pallas_call | solution.py:372
  36.7 0.6 %max.3 = f32[2,1024]{1,0:T(2,128)} maximum(f32[2,1024]{1,0:T(2,128)S(1)} %get-tuple-element.7, f32[2,1024]{1,0:T(2,128)S(1)} %get-tuple-element.8) | non-fusion elementwise | flops 2048 | bytes 24576 | tf_op jit(solution)/shard_map/max | solution.py:406

commit v3 on v2

--- a/solution.py
+++ b/solution.py
@@ -13,7 +13,10 @@
 CHUNK = BLK // ROUNDS
 DIRECT = 64
 RELAY = 32
-SPLIT_ROUNDS = 6
+SPLIT_EVEN = 6
+SPLIT_ODD = 6
+SPEC = 48
+PRE = 1
 OWN = 256
 LINE = 8
 AHEAD = 6
@@ -35,6 +38,9 @@
     send_buf,
     recv_buf,
     relay_buf,
+    pre_buf,
+    spec_buf,
+    client_in,
     meta_out,
     meta_in,
     ret_out,
@@ -50,6 +56,12 @@
     leg1_recv,
     leg2_send,
     leg2_recv,
+    pre_send,
+    pre_recv,
+    spec_send,
+    spec_recv,
+    client_send,
+    client_recv,
 ):
     d = lax.axis_index("dev")
     b = lax.axis_index("band")
@@ -61,6 +73,12 @@
     crosses = jnp.where(c == 1, d < n_dev - 1, d > 0)
     s_cross = jnp.logical_and(is_s, crosses)
     r_cross = jnp.logical_and(is_r, crosses)
+    s_odd = jnp.logical_and(s_cross, odd == 1)
+    r_odd = jnp.logical_and(r_cross, odd == 1)
+    r_even = jnp.logical_and(r_cross, odd == 0)
+    split = jnp.where(odd == 1, SPLIT_ODD, SPLIT_EVEN)
+    skip = jnp.where(odd == 1, PRE, 0)
+    relayed = jnp.where(odd == 1, SPLIT_EVEN, SPLIT_ODD)
     other = d + 1 - 2 * c
     across = jnp.where(crosses, d - 1 + 2 * c, other)
     target = jnp.clip(d + step, 0, n_dev - 1)
@@ -146,6 +164,21 @@
     def _():
         meta_copy.start()
 
+    def client(side):
+        return pltpu.make_async_remote_copy(
+            src_ref=meta_out,
+            dst_ref=client_in.at[side],
+            send_sem=client_send.at[side],
+            recv_sem=client_recv.at[side],
+            device_id=(across, bands[side]),
+            device_id_type=MESH,
+        )
+
+    @pl.when(r_odd)
+    def _():
+        for side in range(2):
+            client(side).start()
+
     def piece(t, start, size):
         return pl.ds(pl.multiple_of(t * CHUNK + start, 16), size)
 
@@ -183,10 +216,58 @@
             device_id_type=MESH,
         )
 
+    def held(t):
+        return pl.ds(pl.multiple_of(t * RELAY, RELAY), RELAY)
+
+    def pre(t, side, k):
+        return pltpu.make_async_remote_copy(
+            src_ref=xn.at[k, relay_rows(t, side)],
+            dst_ref=pre_buf.at[side, k, held(t)],
+            send_sem=pre_send.at[side, k, t],
+            recv_sem=pre_recv.at[side, k, t],
+            device_id=(d, bands[side]),
+            device_id_type=MESH,
+        )
+
+    def spec(k):
+        return pltpu.make_async_remote_copy(
+            src_ref=xn.at[k, pl.ds(0, SPEC)],
+            dst_ref=spec_buf.at[k],
+            send_sem=spec_send.at[k],
+            recv_sem=spec_recv.at[k],
+            device_id=(target, b),
+            device_id_type=MESH,
+        )
+
+    def direct_rest():
+        rows = pl.ds(SPEC, DIRECT - SPEC)
+        return pltpu.make_async_remote_copy(
+            src_ref=send_buf.at[rows],
+            dst_ref=recv_buf.at[rows],
+            send_sem=direct_send.at[0],
+            recv_sem=direct_recv.at[0],
+            device_id=(target, b),
+            device_id_type=MESH,
+        )
+
     def forward(t):
-        for side in range(2):
-            leg1(t, side).wait_recv()
-            leg2(t, side).start()
+        @pl.when(jnp.logical_or(odd == 1, t >= PRE))
+        def _():
+            for side in range(2):
+                leg1(t, side).wait_recv()
+                leg2(t, side).start()
+
+        @pl.when(jnp.logical_and(odd == 0, t < PRE))
+        def _():
+            for side in range(2):
+                for k in range(2):
+                    pre(t, side, k).wait_recv()
+                relay_buf[side, held(t)] = jnp.where(
+                    client_in[side, 0, 0] == 0,
+                    pre_buf[side, 0, held(t)],
+                    pre_buf[side, 1, held(t)],
+                )
+                leg2(t, side).start()
 
     def send(t, index):
         rows = piece(t, 0, CHUNK)
@@ -196,21 +277,30 @@
         def _():
             direct(t, CHUNK).start()
 
-        @pl.when(s_cross)
-        def _():
-            @pl.when(t < SPLIT_ROUNDS)
-            def _():
-                for side in range(2):
-                    leg1(t, side).start()
-                direct(t, DIRECT).start()
-
-            @pl.when(t >= SPLIT_ROUNDS)
-            def _():
-                direct(t, CHUNK).start()
+        @pl.when(jnp.logical_and(s_cross, t >= split))
+        def _():
+            direct(t, CHUNK).start()
+
+        @pl.when(jnp.logical_and(s_cross, jnp.logical_and(t >= skip, t < split)))
+        def _():
+            for side in range(2):
+                leg1(t, side).start()
+
+        @pl.when(jnp.logical_and(jnp.logical_and(s_cross, odd == 0), t < split))
+        def _():
+            direct(t, DIRECT).start()
+
+        @pl.when(jnp.logical_and(s_odd, t == 0))
+        def _():
+            direct_rest().start()
+
+        @pl.when(jnp.logical_and(s_odd, jnp.logical_and(t > 0, t < split)))
+        def _():
+            direct(t, DIRECT).start()
 
     def send_all(index):
         def body(t, carry):
-            @pl.when(t >= early)
+            @pl.when(jnp.logical_and(jnp.logical_not(s_odd), t >= early))
             def _():
                 normalize(t, 0)
 
@@ -233,7 +323,7 @@
         def _():
             own(t, 0)
 
-        @pl.when(jnp.logical_and(r_cross, t < SPLIT_ROUNDS))
+        @pl.when(jnp.logical_and(r_cross, t < relayed))
         def _():
             forward(t)
 
@@ -246,10 +336,37 @@
     def _():
         send_all(local_ref[0])
 
+    def send_both(t, carry):
+        @pl.when(t >= early)
+        def _():
+            normalize(t, 0)
+
+        @pl.when(t == 0)
+        def _():
+            for k in range(2):
+                spec(k).start()
+
+        @pl.when(t < PRE)
+        def _():
+            for side in range(2):
+                for k in range(2):
+                    pre(t, side, k).start()
+
+        return carry
+
+    @pl.when(s_odd)
+    def _():
+        lax.fori_loop(0, ROUNDS, send_both, 0)
+
     @pl.when(odd == 1)
     def _():
         learn()
         send_all(meta_in[0, 0])
+
+    @pl.when(r_even)
+    def _():
+        for side in range(2):
+            client(side).wait_recv()
 
     lax.fori_loop(ahead, ROUNDS, relay, 0)
 
@@ -266,15 +383,25 @@
     keep_live = jnp.where(forwards, before_live, live_ref[0])
 
     def arrive(t):
-        @pl.when(jnp.logical_or(is_s, t >= SPLIT_ROUNDS))
+        @pl.when(jnp.logical_or(is_s, t >= split))
         def _():
             direct(t, CHUNK).wait_recv()
 
-        @pl.when(jnp.logical_and(is_r, t < SPLIT_ROUNDS))
+        @pl.when(jnp.logical_and(is_r, t < split))
+        def _():
+            for side in range(2):
+                leg2(t, side).wait_recv()
+
+        @pl.when(jnp.logical_and(jnp.logical_and(is_r, t < split), jnp.logical_or(odd == 0, t > 0)))
         def _():
             direct(t, DIRECT).wait_recv()
-            for side in range(2):
-                leg2(t, side).wait_recv()
+
+        @pl.when(jnp.logical_and(r_odd, t == 0))
+        def _():
+            for k in range(2):
+                spec(k).wait_recv()
+            direct_rest().wait_recv()
+            recv_buf[:SPEC] = jnp.where(remote_ref[0] == 0, spec_buf[0], spec_buf[1])
 
     def pair(t):
         rows = pl.ds(pl.multiple_of(t * PAIR, PAIR), PAIR)
@@ -342,18 +469,42 @@
     def _():
         ret_copy.wait_send()
 
+    @pl.when(r_odd)
+    def _():
+        for side in range(2):
+            client(side).wait_send()
+
+    @pl.when(s_odd)
+    def _():
+        for k in range(2):
+            spec(k).wait_send()
+        direct_rest().wait_send()
+
     def drain(t, carry):
-        @pl.when(jnp.logical_or(is_r, jnp.logical_and(crosses, t >= SPLIT_ROUNDS)))
+        @pl.when(jnp.logical_or(is_r, jnp.logical_and(crosses, t >= split)))
         def _():
             direct(t, CHUNK).wait_send()
 
-        @pl.when(jnp.logical_and(s_cross, t < SPLIT_ROUNDS))
+        @pl.when(jnp.logical_and(jnp.logical_and(s_cross, odd == 0), t < split))
         def _():
             direct(t, DIRECT).wait_send()
+
+        @pl.when(jnp.logical_and(s_cross, jnp.logical_and(t >= skip, t < split)))
+        def _():
             for side in range(2):
                 leg1(t, side).wait_send()
 
-        @pl.when(jnp.logical_and(r_cross, t < SPLIT_ROUNDS))
+        @pl.when(jnp.logical_and(s_odd, t < PRE))
+        def _():
+            for side in range(2):
+                for k in range(2):
+                    pre(t, side, k).wait_send()
+
+        @pl.when(jnp.logical_and(s_odd, jnp.logical_and(t > 0, t < split)))
+        def _():
+            direct(t, DIRECT).wait_send()
+
+        @pl.when(jnp.logical_and(r_cross, t < relayed))
         def _():
             for side in range(2):
                 leg2(t, side).wait_send()
@@ -380,6 +531,9 @@
                 pltpu.VMEM((BLK, D), jnp.bfloat16),
                 pltpu.VMEM((BLK, D), jnp.bfloat16),
                 pltpu.VMEM((2, ROUNDS * RELAY, D), jnp.bfloat16),
+                pltpu.VMEM((2, 2, PRE * RELAY, D), jnp.bfloat16),
+                pltpu.VMEM((2, SPEC, D), jnp.bfloat16),
+                pltpu.VMEM((2, 8, 128), jnp.int32),
                 pltpu.VMEM((8, 128), jnp.int32),
                 pltpu.VMEM((8, 128), jnp.int32),
                 pltpu.VMEM((ROUNDS, CHUNK), jnp.float32),
@@ -395,6 +549,12 @@
                 dma((2, ROUNDS)),
                 dma((2, ROUNDS)),
                 dma((2, ROUNDS)),
+                dma((2, 2, PRE)),
+                dma((2, 2, PRE)),
+                dma((2,)),
+                dma((2,)),
+                dma((2,)),
+                dma((2,)),
             ],
             compiler_params=pltpu.CompilerParams(
                 collective_id=1, has_side_effects=True, vmem_limit_bytes=52 << 20

time: 37.5 us -> 36.6 us (0.976)
  the two profiles are of different devices: /device:TPU:34 before, /device:TPU:38 now
where the time goes in v3:
time: 36.6 us; the launch traced here: 36.5 us
  Pallas kernels  33.9 us (93%)
  between operations  1.95 us (5%)
  other arithmetic  0.6 us (2%)
    pallas_call x1, Pallas kernels, local(): pl.pallas_call(functools.partial(kernel, n_dev, n_band), out_shape=[jax.S...  33.9 us

profile of v3, /device:TPU:38, one launch (start us, length us, event | category | flops | bytes accessed | tf_op | source)
XLA Modules:
  0.0 36.5 jit_solution(10790309890659362153)
XLA Ops:
  1.9 33.9 %shard_map.46 = (f32[2,1024]{1,0:T(2,128)S(1)}, f32[2,1024]{1,0:T(2,128)S(1)}) custom-call(s32[1]{0:T(128)S(6)} %copy.5.local_ref, s32[1]{0:T(128)S(6)} %copy.6.remote_ref, s32[1]{0:T(128)S(6)} %copy.7.live_ref, bf16[2,1024,1024]{2,1,0:T(8,128)(2,1)} %bitcast.1), custom_call_target="tpu_custom_call" | custom-call | flops 6442450944 | bytes 4194304 | tf_op jit(solution)/shard_map/pallas_call | solution.py:523
  35.9 0.6 %max.3 = f32[2,1024]{1,0:T(2,128)} maximum(f32[2,1024]{1,0:T(2,128)S(1)} %get-tuple-element.7, f32[2,1024]{1,0:T(2,128)S(1)} %get-tuple-element.8) | non-fusion elementwise | flops 2048 | bytes 24576 | tf_op jit(solution)/shard_map/max | solution.py:566

commit v4 on v3

--- a/solution.py
+++ b/solution.py
@@ -444,74 +444,76 @@
     def _():
         ret_copy.start()
 
-    @pl.when(has_target)
-    def _():
-        ret_copy.wait_recv()
-
-    @pl.when(jnp.logical_not(has_target))
-    def _():
-        ret_in[...] = jnp.full(ret_in.shape, -2.0, jnp.float32)
-
     kept = jnp.max(pair_acc[...], axis=0, keepdims=True)
     kept = jnp.where(keep_live > 0, kept, -2.0)
+    for k in range(2):
+        best = jnp.max(own_acc[k], axis=0, keepdims=True)
+        best_ref[k : k + 1] = jnp.maximum(best, jnp.where(keep_index == k, kept, -2.0))
+
+    @pl.when(d < n_dev - 1)
+    def _():
+        meta_copy.wait_send()
+
+    @pl.when(r_odd)
+    def _():
+        for side in range(2):
+            client(side).wait_send()
+
+    @pl.when(s_odd)
+    def _():
+        for k in range(2):
+            spec(k).wait_send()
+        direct_rest().wait_send()
+
+    def drain(t, carry):
+        @pl.when(jnp.logical_or(is_r, jnp.logical_and(crosses, t >= split)))
+        def _():
+            direct(t, CHUNK).wait_send()
+
+        @pl.when(jnp.logical_and(jnp.logical_and(s_cross, odd == 0), t < split))
+        def _():
+            direct(t, DIRECT).wait_send()
+
+        @pl.when(jnp.logical_and(s_cross, jnp.logical_and(t >= skip, t < split)))
+        def _():
+            for side in range(2):
+                leg1(t, side).wait_send()
+
+        @pl.when(jnp.logical_and(s_odd, t < PRE))
+        def _():
+            for side in range(2):
+                for k in range(2):
+                    pre(t, side, k).wait_send()
+
+        @pl.when(jnp.logical_and(s_odd, jnp.logical_and(t > 0, t < split)))
+        def _():
+            direct(t, DIRECT).wait_send()
+
+        @pl.when(jnp.logical_and(r_cross, t < relayed))
+        def _():
+            for side in range(2):
+                leg2(t, side).wait_send()
+
+        return carry
+
+    lax.fori_loop(0, ROUNDS, drain, 0)
+
+    @pl.when(has_target)
+    def _():
+        ret_copy.wait_recv()
+
+    @pl.when(jnp.logical_not(has_target))
+    def _():
+        ret_in[...] = jnp.full(ret_in.shape, -2.0, jnp.float32)
+
     sent = jnp.concatenate([ret_in[t : t + 1] for t in range(ROUNDS)], axis=1)
     sent = jnp.where(send_live > 0, sent, -2.0)
     for k in range(2):
-        best = jnp.max(own_acc[k], axis=0, keepdims=True)
-        best_ref[k : k + 1] = jnp.maximum(best, jnp.where(keep_index == k, kept, -2.0))
         sent_ref[k : k + 1] = jnp.where(send_index == k, sent, -2.0)
 
-    @pl.when(d < n_dev - 1)
-    def _():
-        meta_copy.wait_send()
-
     @pl.when(has_source)
     def _():
         ret_copy.wait_send()
-
-    @pl.when(r_odd)
-    def _():
-        for side in range(2):
-            client(side).wait_send()
-
-    @pl.when(s_odd)
-    def _():
-        for k in range(2):
-            spec(k).wait_send()
-        direct_rest().wait_send()
-
-    def drain(t, carry):
-        @pl.when(jnp.logical_or(is_r, jnp.logical_and(crosses, t >= split)))
-        def _():
-            direct(t, CHUNK).wait_send()
-
-        @pl.when(jnp.logical_and(jnp.logical_and(s_cross, odd == 0), t < split))
-        def _():
-            direct(t, DIRECT).wait_send()
-
-        @pl.when(jnp.logical_and(s_cross, jnp.logical_and(t >= skip, t < split)))
-        def _():
-            for side in range(2):
-                leg1(t, side).wait_send()
-
-        @pl.when(jnp.logical_and(s_odd, t < PRE))
-        def _():
-            for side in range(2):
-                for k in range(2):
-                    pre(t, side, k).wait_send()
-
-        @pl.when(jnp.logical_and(s_odd, jnp.logical_and(t > 0, t < split)))
-        def _():
-            direct(t, DIRECT).wait_send()
-
-        @pl.when(jnp.logical_and(r_cross, t < relayed))
-        def _():
-            for side in range(2):
-                leg2(t, side).wait_send()
-
-        return carry
-
-    lax.fori_loop(0, ROUNDS, drain, 0)
 
 
 def solution(mesh):

time: 36.6 us -> 36.3 us (level)
  no operation moved by 1% of the time
where the time goes in v4:
time: 36.3 us; the launch traced here: 36.2 us
  Pallas kernels  33.6 us (93%)
  between operations  1.95 us (5%)
  other arithmetic  0.6 us (2%)
    pallas_call x1, Pallas kernels, local(): pl.pallas_call(functools.partial(kernel, n_dev, n_band), out_shape=[jax.S...  33.6 us

profile of v4, /device:TPU:38, one launch (start us, length us, event | category | flops | bytes accessed | tf_op | source)
XLA Modules:
  0.0 36.2 jit_solution(8179534124494816022)
XLA Ops:
  1.9 33.6 %shard_map.46 = (f32[2,1024]{1,0:T(2,128)S(1)}, f32[2,1024]{1,0:T(2,128)S(1)}) custom-call(s32[1]{0:T(128)S(6)} %copy.5.local_ref, s32[1]{0:T(128)S(6)} %copy.6.remote_ref, s32[1]{0:T(128)S(6)} %copy.7.live_ref, bf16[2,1024,1024]{2,1,0:T(8,128)(2,1)} %bitcast.1), custom_call_target="tpu_custom_call" | custom-call | flops 6442450944 | bytes 4194304 | tf_op jit(solution)/shard_map/pallas_call | solution.py:525
  35.6 0.6 %max.3 = f32[2,1024]{1,0:T(2,128)} maximum(f32[2,1024]{1,0:T(2,128)S(1)} %get-tuple-element.7, f32[2,1024]{1,0:T(2,128)S(1)} %get-tuple-element.8) | non-fusion elementwise | flops 2048 | bytes 24576 | tf_op jit(solution)/shard_map/max | solution.py:568
